TPU v7x, 32 devices: a whole 2x2x4 slice. The times are simulated.
32 devices in a mesh: groups: 2 (over y), leaf: 4 (over z), sub: 2 (over x), vec: 2 (over core).
Axes of the slice: x: 2, y: 2, z: 4, core: 2. Of those that a mesh axis runs over, the one named last changes fastest.
Arguments:
- vectors: bfloat16 [32, 131072], P('vec', ('groups', 'leaf', 'sub')), parts along dimension 1, may hold values from -6 to 6
- points: float32 [3, 131072], P(None, ('groups', 'leaf', 'sub')), parts along dimension 1, as said below
- leaf_basis: bfloat16 [32, 131072], P(None, ('groups', 'leaf', 'sub')), parts along dimension 1, may hold values from -0.75 to 0.75
- transfer: float32 [8, 32, 32], replicated, may hold values from -1 to 1
- proxy_points: float32 [3, 32], replicated, may hold values from -0.5 to 0.5
- near_list: int32 [2048, 27], P(('groups', 'leaf', 'sub')), parts along dimension 0, may hold values from -1 to 1023, as said below
- far_leaf: int32 [2048, 64], P(('groups', 'leaf', 'sub')), parts along dimension 0, may hold values from -1 to 1023, as said below
- far_mid: int32 [256, 12], P(('groups', 'leaf', 'sub')), parts along dimension 0, may hold values from -1 to 127, as said below
- far_root: int32 [32, 3], P(('groups', 'leaf', 'sub')), parts along dimension 0, may hold values from -1 to 15, as said below
- far_top: int32 [8, 3], P('groups'), parts along dimension 0, may hold values from -1 to 3, as said below
Outputs:
- field: float32 [32, 131072], P('vec', ('groups', 'leaf', 'sub')), parts along dimension 1
There are 2 independent parts, one for each index of `groups`. A program takes and returns all parts, laid end to end along the dimension named above; an argument that names none is the same for every part. Nothing has to cross between parts.
Inputs may be any that keep to these rules, and one draw needn't show every extreme that they name: The points of leaf i lie in the unit cube whose corner is leaf i's cell in Morton order. `near_list`: entry 0 of row i is i; every other entry is -1 or a leaf whose cell touches leaf i's cell (by a face, an edge or a corner) and whose index differs from i by 1 to 127, each named once in a row; -1 entries stand after all others. `far_leaf`: each entry is -1 or a leaf whose index differs from the row's by 1 to 127; -1 entries stand after all others. `far_mid`: each entry is -1 or a mid node whose index differs from the row's by 1 to 15; -1 entries stand after all others. `far_root`: each entry is -1 or another root below the same top node, each named once in a row; -1 entries stand after all others. `far_top`: each entry is -1 or another top node, each named once in a row; -1 entries stand after all others.
All inputs are finite; a program needn't handle non-finite values.
Results may differ from a plain program's by a relative error of at most 0.0027.
The roundings to bfloat16 on the way count: a program that leaves them out, or rounds other values in their place, can miss the bound.
Values may be sent and summed in bfloat16 or wider, within the bound.
No kernel may reach another device: no remote copies, remote signals or barrier semaphores. Data moves between devices by JAX's collectives and lax.ppermute only.
A program may use at most 64 MiB of HBM per device.

v0:
```python
import math

import jax
import jax.numpy as jnp
import numpy as np
from jax import lax
from jax.sharding import PartitionSpec as P

SOFTENING = 0.25
INV_FOUR_PI = 0.25 / math.pi


def with_halo(block, sides, width):
    for axis, dim in sides:
        count = lax.axis_size(axis)
        forward = [(i, i + 1) for i in range(count - 1)]
        backward = [(target, source) for source, target in forward]
        low = lax.ppermute(
            lax.slice_in_dim(block, block.shape[dim] - width, None, axis=dim), axis, forward
        )
        high = lax.ppermute(lax.slice_in_dim(block, 0, width, axis=dim), axis, backward)
        block = jnp.concatenate([low, block, high], axis=dim)
    return block


def pair_kernel(squared):
    return INV_FOUR_PI / jnp.sqrt(squared + SOFTENING * SOFTENING)


def near_field(window_values, window_points, target_points, partner_lists, shift_rows):
    channels = window_values.shape[0]
    targets = partner_lists.shape[0]
    slot_count = partner_lists.shape[1]
    per_leaf = target_points.shape[1] // targets
    source_values = window_values.reshape(channels, -1, per_leaf)
    source_points = window_points.reshape(3, -1, per_leaf)
    block_size = min(targets, max(16, targets // 16))
    turn_count = targets // block_size
    target_blocks = target_points.reshape(3, turn_count, block_size, per_leaf).transpose(1, 0, 2, 3)
    list_blocks = partner_lists.reshape(turn_count, block_size, slot_count)

    def near_one_block(operands):
        target_block, list_block = operands
        present = list_block >= 0
        local_rows = jnp.where(present, list_block - shift_rows, 0)
        gathered = source_points[:, local_rows].reshape(3, block_size, 1, slot_count * per_leaf)
        squared = jnp.zeros((block_size, per_leaf, slot_count * per_leaf), jnp.float32)
        for component in range(3):
            offset = target_block[component][:, :, None] - gathered[component]
            squared = squared + offset * offset
        weight_mask = jnp.repeat(present.astype(jnp.float32), per_leaf, axis=1)[:, None, :]
        weights = (pair_kernel(squared) * weight_mask).astype(jnp.bfloat16)
        values = source_values[:, local_rows].reshape(channels, block_size, slot_count * per_leaf)
        return jnp.einsum("bpm,wbm->wbp", weights, values, preferred_element_type=jnp.float32)

    results = lax.map(near_one_block, (target_blocks, list_blocks))
    return results.transpose(1, 0, 2, 3).reshape(channels, targets * per_leaf)


def couple(coefficients, centres, own_centres, partner_lists, shift_rows, radius, proxy_points):
    node_count, slot_count = partner_lists.shape
    rank_width = proxy_points.shape[1]
    block_size = min(node_count, 16)
    turn_count = node_count // block_size
    own_blocks = own_centres.reshape(3, turn_count, block_size).transpose(1, 0, 2)
    list_blocks = partner_lists.reshape(turn_count, block_size, slot_count)

    def couple_one_block(operands):
        own_block, list_block = operands
        present = list_block >= 0
        local_rows = jnp.where(present, list_block - shift_rows, 0)
        far_centres = centres[:, local_rows]
        squared = jnp.zeros((block_size, slot_count, rank_width, rank_width), jnp.float32)
        for component in range(3):
            target = (
                own_block[component][:, None, None]
                + radius * proxy_points[component][None, None, :]
            )
            source = (
                far_centres[component][:, :, None] + radius * proxy_points[component][None, None, :]
            )
            offset = target[:, :, :, None] - source[:, :, None, :]
            squared = squared + offset * offset
        weights = pair_kernel(squared) * present.astype(jnp.float32)[:, :, None, None]
        return jnp.einsum(
            "bfrs,bfsv->brv", weights, coefficients[local_rows], precision=lax.Precision.HIGHEST
        )

    results = lax.map(couple_one_block, (own_blocks, list_blocks))
    return results.reshape(node_count, rank_width, -1)


def upward(children, matrices):
    branch = matrices.shape[0]
    grouped = children.reshape(-1, branch, children.shape[1], children.shape[2])
    return jnp.einsum("csr,ncsv->nrv", matrices, grouped, precision=lax.Precision.HIGHEST)


def downward(parents, matrices):
    spread = jnp.einsum("crs,nsv->ncrv", matrices, parents, precision=lax.Precision.HIGHEST)
    return spread.reshape(-1, parents.shape[1], parents.shape[2])


def body(
    vectors,
    points,
    leaf_basis,
    transfer,
    proxy_points,
    near_list,
    far_leaf,
    far_mid,
    far_root,
    far_top,
):
    leaf_count = near_list.shape[0]
    mid_count = far_mid.shape[0]
    root_count = far_root.shape[0]
    per_leaf = points.shape[1] // leaf_count
    rank_width = leaf_basis.shape[0]
    vec_width = vectors.shape[0]
    device = lax.axis_index(("leaf", "sub"))
    leaf_base = device * leaf_count
    mid_base = device * mid_count
    basis_blocks = leaf_basis.reshape(rank_width, leaf_count, per_leaf)
    leaf_coef = jnp.einsum(
        "rlp,vlp->lrv",
        basis_blocks,
        vectors.reshape(vec_width, leaf_count, per_leaf),
        preferred_element_type=jnp.float32,
    )
    mid_coef = upward(leaf_coef, transfer)
    root_coef = upward(mid_coef, transfer)
    window_points = with_halo(points, ((("leaf", "sub"), 1),), points.shape[1])
    window = with_halo(vectors, ((("leaf", "sub"), 1),), points.shape[1])
    near_part = near_field(window, window_points, points, near_list, leaf_base - leaf_count)
    window_leaf_centre = jnp.mean(window_points.reshape(3, 3 * leaf_count, per_leaf), axis=2)
    window_mid_centre = jnp.mean(window_leaf_centre.reshape(3, -1, 8), axis=2)
    leaf_centre = window_leaf_centre[:, leaf_count : 2 * leaf_count]
    mid_centre = window_mid_centre[:, mid_count : 2 * mid_count]
    root_centre = jnp.mean(mid_centre.reshape(3, -1, 8), axis=2)
    stacked = jnp.concatenate([leaf_coef, mid_coef], axis=0).reshape(
        leaf_count + mid_count, rank_width * vec_width
    )
    coef_window = with_halo(stacked, ((("leaf", "sub"), 0),), leaf_count + mid_count)
    coef_window = coef_window.reshape(3, leaf_count + mid_count, rank_width, vec_width)
    leaf_window = coef_window[:, :leaf_count].reshape(3 * leaf_count, rank_width, vec_width)
    mid_window = coef_window[:, leaf_count:].reshape(3 * mid_count, rank_width, vec_width)
    row_size = lax.axis_size("sub") * root_count
    top_table = transfer[np.arange(row_size) % 8]
    root_flat = root_coef.reshape(root_count, rank_width * vec_width)
    top_index = lax.axis_index("leaf")
    all_roots, all_centres = (
        lax.all_gather(root_flat, ("leaf", "sub"), axis=0, tiled=True),
        lax.all_gather(root_centre, ("leaf", "sub"), axis=1, tiled=True),
    )
    all_roots = all_roots.reshape(-1, rank_width, vec_width)
    top_coef = upward(all_roots, top_table)
    top_centre = jnp.mean(all_centres.reshape(3, -1, row_size), axis=2)
    sibling_shift = 0
    this_top_centre = lax.dynamic_slice_in_dim(top_centre, top_index, 1, 1)
    this_top_list = lax.dynamic_slice_in_dim(far_top, top_index, 1, 0)
    top_out = couple(top_coef, top_centre, this_top_centre, this_top_list, 0, 8.0, proxy_points)
    root_far = couple(
        all_roots, all_centres, root_centre, far_root, sibling_shift, 4.0, proxy_points
    )
    position = lax.axis_index("sub") * root_count + jnp.arange(root_count, dtype=jnp.int32)
    selector = (jnp.arange(8, dtype=jnp.int32)[None, :] == (position % 8)[:, None]).astype(
        jnp.float32
    )
    root_table = jnp.einsum("kc,crs->krs", selector, transfer, precision=lax.Precision.HIGHEST)
    root_out = root_far + jnp.einsum(
        "krs,sv->krv", root_table, top_out[0], precision=lax.Precision.HIGHEST
    )
    mid_out = couple(
        mid_window, window_mid_centre, mid_centre, far_mid, mid_base - mid_count, 2.0, proxy_points
    ) + downward(root_out, transfer)
    leaf_out = couple(
        leaf_window,
        window_leaf_centre,
        leaf_centre,
        far_leaf,
        leaf_base - leaf_count,
        1.0,
        proxy_points,
    ) + downward(mid_out, transfer)
    coarse = leaf_out.astype(jnp.bfloat16)
    far_part = jnp.einsum(
        "rlp,lrv->vlp", basis_blocks, coarse, preferred_element_type=jnp.float32
    ).reshape(vec_width, -1)
    return near_part + far_part


def solution(mesh):
    return jax.shard_map(
        body,
        mesh=mesh,
        in_specs=(
            P("vec", ("groups", "leaf", "sub")),
            P(None, ("groups", "leaf", "sub")),
            P(None, ("groups", "leaf", "sub")),
            P(),
            P(),
            P(("groups", "leaf", "sub"), None),
            P(("groups", "leaf", "sub"), None),
            P(("groups", "leaf", "sub"), None),
            P(("groups", "leaf", "sub"), None),
            P("groups", None),
        ),
        out_specs=P("vec", ("groups", "leaf", "sub")),
        check_vma=False,
    )
```

profile of v0, /device:TPU:0, one launch (start us, length us, event | category | flops | bytes accessed | tf_op | source)
XLA Modules:
  0.0 601.2 jit_solution(714563444369647561)
XLA Ops:
  1.4 5.5 collective-permute-start
  8.2 6.1 %collective-permute-start.2 = (f32[3,8192]{1,0:T(4,128)}, f32[3,8192]{1,0:T(4,128)}, u32[]{:S(2)}, u32[]{:S(2)}) collective-permute-start(f32[3,8192]{1,0:T(4,128)} %param.17), channel_id=1, source_target_pairs={{0,2},{2,4},{4,6},{6,8},{8,10},{10,12},{12,14},{1,3},{3,5},{5,7},{... | collective-permute-start | bytes 294920 | tf_op jit(solution)/shard_map/ppermute | solution.py:18
  24.2 36.2 %all-gather.1 = f32[8,2,512]{2,1,0:T(2,128)S(1)} all-gather(f32[1,2,512]{2,1,0:T(2,128)S(1)} %reshape.971), channel_id=1, replica_groups=mesh['groups'=2,'leaf'=4,'sub'=2,'vec'=2] {'leaf','sub'}, dimensions={0}, use_global_device_ids=true | all-gather | bytes 36864 | tf_op jit(solution)/shard_map/all_gather | solution.py:154
  72.0 18.6 %all-gather = f32[8,2,3]{2,1,0:T(2,128)S(1)} all-gather(f32[1,2,3]{2,1,0:T(2,128)S(1)} %bitcast.283), channel_id=1, replica_groups=mesh['groups'=2,'leaf'=4,'sub'=2,'vec'=2] {'leaf','sub'}, dimensions={0}, use_global_device_ids=true | all-gather | bytes 216 | tf_op jit(solution)/shard_map/all_gather | solution.py:155
  106.8 158.4 %while.4 = (s32[]{:T(128)}, f32[8,16,16,64]{3,1,2,0:T(8,128)}, s32[8,16,27]{2,1,0:T(8,128)}, s32[]{:T(128)}, bf16[16,384,64]{2,0,1:T(8,128)(2,1)S(1)}, /*index=5...) while((s32[]{:T(128)}, f32[8,16,16,64]{3,1,2,0:T(8,128)}, s32[8,16,27]{2,1,0:T(8,128)}, s32[]{:T(128)}, ...), condition=%wide.region_1.2_spmd, body=%wide.region_0.1_spmd.sunk | while | flops 76091344 | bytes 14563209 | solution.py:56
  161.0 5.2 fusion.150
  240.2 5.2 fusion.150
  282.8 313.2 %while.5 = (s32[]{:T(128)}, f32[8,16,32,16]{2,3,1,0:T(8,128)}, f32[8,3,16]{2,1,0:T(4,128)}, f32[3,32]{1,0:T(4,128)S(1)}, s32[8,16,64]{2,1,0:T(8,128)}, /*index=5...) while((s32[]{:T(128)}, f32[8,16,32,16]{2,3,1,0:T(8,128)}, f32[8,3,16]{2,1,0:T(4,128)}, ...), condition=%wide.region_4.5_spmd, body=%wide.region_3.4_spmd.sunk | while | flops 211920384 | bytes 13648441 | solution.py:89
  284.3 10.5 %gather_fusion.2 = f32[1024,32,16]{1,2,0:T(8,128)} fusion(f32[384,32,16]{1,2,0:T(8,128)S(1)} %get-tuple-element.494, s32[1024]{0:T(1024)S(1)} %broadcast_clamp_fusion.2), kind=kCustom, calls=%fused_computation.3.clone.1 | custom fusion | bytes 4198400 | tf_op jit(solution)/shard_map/while/body/eval_jaxpr/gather | solution.py:86
  294.8 7.6 %copy.198 = f32[16,64,32,16]{1,3,2,0:T(8,128)} copy(f32[16,64,32,16]{2,3,1,0:T(8,128)} %bitcast.261) | data formatting | bytes 4194304 | tf_op jit(solution)/shard_map/while/body/eval_jaxpr/gather | solution.py:86
  308.8 13.2 %fusion.153 = f32[8,16,32,16]{2,3,1,0:T(8,128)} fusion(f32[8,16,32,16]{2,3,1,0:T(8,128)} %get-tuple-element.479, s32[]{:T(128)S(6)} %copy.210, f32[16,64,32,16]{1,3,2,0:T(8,128)} %copy.198, f32[16,64]{1,0:T(8,128)S(1)} %get-tuple-element.431, f32[16,64,32]{1,2,0:T(8,128)S(1)} %get-tuple-element.436, f32[16,32]{1,0:T(8,128)S(1)} %get-tuple-element.439, ...), kind=kOutput, calls=%fused_computation.46.clone.1 | convolution fusion | flops 211812352 | bytes 4728836 | tf_op jit(solution)/shard_map/while/body/eval_jaxpr/bfrs,bfsv->brv/dot_general | solution.py:85
  323.4 10.5 %gather_fusion.2 = f32[1024,32,16]{1,2,0:T(8,128)} fusion(f32[384,32,16]{1,2,0:T(8,128)S(1)} %get-tuple-element.494, s32[1024]{0:T(1024)S(1)} %broadcast_clamp_fusion.2), kind=kCustom, calls=%fused_computation.3.clone.1 | custom fusion | bytes 4198400 | tf_op jit(solution)/shard_map/while/body/eval_jaxpr/gather | solution.py:86
  334.0 7.6 %copy.198 = f32[16,64,32,16]{1,3,2,0:T(8,128)} copy(f32[16,64,32,16]{2,3,1,0:T(8,128)} %bitcast.261) | data formatting | bytes 4194304 | tf_op jit(solution)/shard_map/while/body/eval_jaxpr/gather | solution.py:86
  347.9 13.2 %fusion.153 = f32[8,16,32,16]{2,3,1,0:T(8,128)} fusion(f32[8,16,32,16]{2,3,1,0:T(8,128)} %get-tuple-element.479, s32[]{:T(128)S(6)} %copy.210, f32[16,64,32,16]{1,3,2,0:T(8,128)} %copy.198, f32[16,64]{1,0:T(8,128)S(1)} %get-tuple-element.431, f32[16,64,32]{1,2,0:T(8,128)S(1)} %get-tuple-element.436, f32[16,32]{1,0:T(8,128)S(1)} %get-tuple-element.439, ...), kind=kOutput, calls=%fused_computation.46.clone.1 | convolution fusion | flops 211812352 | bytes 4728836 | tf_op jit(solution)/shard_map/while/body/eval_jaxpr/bfrs,bfsv->brv/dot_general | solution.py:85
  362.6 10.5 %gather_fusion.2 = f32[1024,32,16]{1,2,0:T(8,128)} fusion(f32[384,32,16]{1,2,0:T(8,128)S(1)} %get-tuple-element.494, s32[1024]{0:T(1024)S(1)} %broadcast_clamp_fusion.2), kind=kCustom, calls=%fused_computation.3.clone.1 | custom fusion | bytes 4198400 | tf_op jit(solution)/shard_map/while/body/eval_jaxpr/gather | solution.py:86
  373.2 7.6 %copy.198 = f32[16,64,32,16]{1,3,2,0:T(8,128)} copy(f32[16,64,32,16]{2,3,1,0:T(8,128)} %bitcast.261) | data formatting | bytes 4194304 | tf_op jit(solution)/shard_map/while/body/eval_jaxpr/gather | solution.py:86
  387.0 13.2 %fusion.153 = f32[8,16,32,16]{2,3,1,0:T(8,128)} fusion(f32[8,16,32,16]{2,3,1,0:T(8,128)} %get-tuple-element.479, s32[]{:T(128)S(6)} %copy.210, f32[16,64,32,16]{1,3,2,0:T(8,128)} %copy.198, f32[16,64]{1,0:T(8,128)S(1)} %get-tuple-element.431, f32[16,64,32]{1,2,0:T(8,128)S(1)} %get-tuple-element.436, f32[16,32]{1,0:T(8,128)S(1)} %get-tuple-element.439, ...), kind=kOutput, calls=%fused_computation.46.clone.1 | convolution fusion | flops 211812352 | bytes 4728836 | tf_op jit(solution)/shard_map/while/body/eval_jaxpr/bfrs,bfsv->brv/dot_general | solution.py:85
  401.7 10.5 %gather_fusion.2 = f32[1024,32,16]{1,2,0:T(8,128)} fusion(f32[384,32,16]{1,2,0:T(8,128)S(1)} %get-tuple-element.494, s32[1024]{0:T(1024)S(1)} %broadcast_clamp_fusion.2), kind=kCustom, calls=%fused_computation.3.clone.1 | custom fusion | bytes 4198400 | tf_op jit(solution)/shard_map/while/body/eval_jaxpr/gather | solution.py:86
  412.3 7.6 %copy.198 = f32[16,64,32,16]{1,3,2,0:T(8,128)} copy(f32[16,64,32,16]{2,3,1,0:T(8,128)} %bitcast.261) | data formatting | bytes 4194304 | tf_op jit(solution)/shard_map/while/body/eval_jaxpr/gather | solution.py:86
  426.2 13.2 %fusion.153 = f32[8,16,32,16]{2,3,1,0:T(8,128)} fusion(f32[8,16,32,16]{2,3,1,0:T(8,128)} %get-tuple-element.479, s32[]{:T(128)S(6)} %copy.210, f32[16,64,32,16]{1,3,2,0:T(8,128)} %copy.198, f32[16,64]{1,0:T(8,128)S(1)} %get-tuple-element.431, f32[16,64,32]{1,2,0:T(8,128)S(1)} %get-tuple-element.436, f32[16,32]{1,0:T(8,128)S(1)} %get-tuple-element.439, ...), kind=kOutput, calls=%fused_computation.46.clone.1 | convolution fusion | flops 211812352 | bytes 4728836 | tf_op jit(solution)/shard_map/while/body/eval_jaxpr/bfrs,bfsv->brv/dot_general | solution.py:85
  440.9 10.5 %gather_fusion.2 = f32[1024,32,16]{1,2,0:T(8,128)} fusion(f32[384,32,16]{1,2,0:T(8,128)S(1)} %get-tuple-element.494, s32[1024]{0:T(1024)S(1)} %broadcast_clamp_fusion.2), kind=kCustom, calls=%fused_computation.3.clone.1 | custom fusion | bytes 4198400 | tf_op jit(solution)/shard_map/while/body/eval_jaxpr/gather | solution.py:86
  451.4 7.6 %copy.198 = f32[16,64,32,16]{1,3,2,0:T(8,128)} copy(f32[16,64,32,16]{2,3,1,0:T(8,128)} %bitcast.261) | data formatting | bytes 4194304 | tf_op jit(solution)/shard_map/while/body/eval_jaxpr/gather | solution.py:86
  465.4 13.2 %fusion.153 = f32[8,16,32,16]{2,3,1,0:T(8,128)} fusion(f32[8,16,32,16]{2,3,1,0:T(8,128)} %get-tuple-element.479, s32[]{:T(128)S(6)} %copy.210, f32[16,64,32,16]{1,3,2,0:T(8,128)} %copy.198, f32[16,64]{1,0:T(8,128)S(1)} %get-tuple-element.431, f32[16,64,32]{1,2,0:T(8,128)S(1)} %get-tuple-element.436, f32[16,32]{1,0:T(8,128)S(1)} %get-tuple-element.439, ...), kind=kOutput, calls=%fused_computation.46.clone.1 | convolution fusion | flops 211812352 | bytes 4728836 | tf_op jit(solution)/shard_map/while/body/eval_jaxpr/bfrs,bfsv->brv/dot_general | solution.py:85
  480.0 10.5 %gather_fusion.2 = f32[1024,32,16]{1,2,0:T(8,128)} fusion(f32[384,32,16]{1,2,0:T(8,128)S(1)} %get-tuple-element.494, s32[1024]{0:T(1024)S(1)} %broadcast_clamp_fusion.2), kind=kCustom, calls=%fused_computation.3.clone.1 | custom fusion | bytes 4198400 | tf_op jit(solution)/shard_map/while/body/eval_jaxpr/gather | solution.py:86
  490.6 7.6 %copy.198 = f32[16,64,32,16]{1,3,2,0:T(8,128)} copy(f32[16,64,32,16]{2,3,1,0:T(8,128)} %bitcast.261) | data formatting | bytes 4194304 | tf_op jit(solution)/shard_map/while/body/eval_jaxpr/gather | solution.py:86
  504.5 13.2 %fusion.153 = f32[8,16,32,16]{2,3,1,0:T(8,128)} fusion(f32[8,16,32,16]{2,3,1,0:T(8,128)} %get-tuple-element.479, s32[]{:T(128)S(6)} %copy.210, f32[16,64,32,16]{1,3,2,0:T(8,128)} %copy.198, f32[16,64]{1,0:T(8,128)S(1)} %get-tuple-element.431, f32[16,64,32]{1,2,0:T(8,128)S(1)} %get-tuple-element.436, f32[16,32]{1,0:T(8,128)S(1)} %get-tuple-element.439, ...), kind=kOutput, calls=%fused_computation.46.clone.1 | convolution fusion | flops 211812352 | bytes 4728836 | tf_op jit(solution)/shard_map/while/body/eval_jaxpr/bfrs,bfsv->brv/dot_general | solution.py:85
  519.2 10.5 %gather_fusion.2 = f32[1024,32,16]{1,2,0:T(8,128)} fusion(f32[384,32,16]{1,2,0:T(8,128)S(1)} %get-tuple-element.494, s32[1024]{0:T(1024)S(1)} %broadcast_clamp_fusion.2), kind=kCustom, calls=%fused_computation.3.clone.1 | custom fusion | bytes 4198400 | tf_op jit(solution)/shard_map/while/body/eval_jaxpr/gather | solution.py:86
  529.7 7.6 %copy.198 = f32[16,64,32,16]{1,3,2,0:T(8,128)} copy(f32[16,64,32,16]{2,3,1,0:T(8,128)} %bitcast.261) | data formatting | bytes 4194304 | tf_op jit(solution)/shard_map/while/body/eval_jaxpr/gather | solution.py:86
  543.6 13.2 %fusion.153 = f32[8,16,32,16]{2,3,1,0:T(8,128)} fusion(f32[8,16,32,16]{2,3,1,0:T(8,128)} %get-tuple-element.479, s32[]{:T(128)S(6)} %copy.210, f32[16,64,32,16]{1,3,2,0:T(8,128)} %copy.198, f32[16,64]{1,0:T(8,128)S(1)} %get-tuple-element.431, f32[16,64,32]{1,2,0:T(8,128)S(1)} %get-tuple-element.436, f32[16,32]{1,0:T(8,128)S(1)} %get-tuple-element.439, ...), kind=kOutput, calls=%fused_computation.46.clone.1 | convolution fusion | flops 211812352 | bytes 4728836 | tf_op jit(solution)/shard_map/while/body/eval_jaxpr/bfrs,bfsv->brv/dot_general | solution.py:85
  558.3 10.5 %gather_fusion.2 = f32[1024,32,16]{1,2,0:T(8,128)} fusion(f32[384,32,16]{1,2,0:T(8,128)S(1)} %get-tuple-element.494, s32[1024]{0:T(1024)S(1)} %broadcast_clamp_fusion.2), kind=kCustom, calls=%fused_computation.3.clone.1 | custom fusion | bytes 4198400 | tf_op jit(solution)/shard_map/while/body/eval_jaxpr/gather | solution.py:86
  568.9 7.6 %copy.198 = f32[16,64,32,16]{1,3,2,0:T(8,128)} copy(f32[16,64,32,16]{2,3,1,0:T(8,128)} %bitcast.261) | data formatting | bytes 4194304 | tf_op jit(solution)/shard_map/while/body/eval_jaxpr/gather | solution.py:86
  582.8 13.2 %fusion.153 = f32[8,16,32,16]{2,3,1,0:T(8,128)} fusion(f32[8,16,32,16]{2,3,1,0:T(8,128)} %get-tuple-element.479, s32[]{:T(128)S(6)} %copy.210, f32[16,64,32,16]{1,3,2,0:T(8,128)} %copy.198, f32[16,64]{1,0:T(8,128)S(1)} %get-tuple-element.431, f32[16,64,32]{1,2,0:T(8,128)S(1)} %get-tuple-element.436, f32[16,32]{1,0:T(8,128)S(1)} %get-tuple-element.439, ...), kind=kOutput, calls=%fused_computation.46.clone.1 | convolution fusion | flops 211812352 | bytes 4728836 | tf_op jit(solution)/shard_map/while/body/eval_jaxpr/bfrs,bfsv->brv/dot_general | solution.py:85
  (436 shorter events, 272.2 us)
Async XLA Ops:
  0.0 19.4 %copy-start = (f32[8,32,32]{2,1,0:T(8,128)S(1)}, f32[8,32,32]{2,1,0:T(8,128)}, u32[]{:S(2)}) copy-start(f32[8,32,32]{2,1,0:T(8,128)} %param.19) | copy-start | bytes 98308
  0.0 103.8 %collective-permute-start.1 = (bf16[16,8192]{1,0:T(8,128)(2,1)}, bf16[16,8192]{1,0:T(8,128)(2,1)S(1)}, u32[]{:S(2)}, u32[]{:S(2)}) collective-permute-start(bf16[16,8192]{1,0:T(8,128)(2,1)} %param.16), channel_id=1, source_target_pairs={{2,0},{4,2},{6,4},{8,6},{10,8},{12,10},{14,12},{3,1},{5,3},{7,5},{... | collective-permute-start | bytes 786440 | tf_op jit(solution)/shard_map/ppermute | solution.py:21
  1.4 102.3 %collective-permute-start = (bf16[16,8192]{1,0:T(8,128)(2,1)}, bf16[16,8192]{1,0:T(8,128)(2,1)S(1)}, u32[]{:S(2)}, u32[]{:S(2)}) collective-permute-start(bf16[16,8192]{1,0:T(8,128)(2,1)} %param.16), channel_id=1, source_target_pairs={{0,2},{2,4},{4,6},{6,8},{8,10},{10,12},{12,14},{1,3},{3,5},{5,7},{... | collective-permute-start | bytes 786440 | tf_op jit(solution)/shard_map/ppermute | solution.py:18
  6.9 60.0 %collective-permute-start.3 = (f32[3,8192]{1,0:T(4,128)}, f32[3,8192]{1,0:T(4,128)S(1)}, u32[]{:S(2)}, u32[]{:S(2)}) collective-permute-start(f32[3,8192]{1,0:T(4,128)} %param.17), channel_id=1, source_target_pairs={{2,0},{4,2},{6,4},{8,6},{10,8},{12,10},{14,12},{3,1},{5,3},{7,5},{... | collective-permute-start | bytes 294920 | tf_op jit(solution)/shard_map/ppermute | solution.py:21
  8.2 61.6 %collective-permute-start.2 = (f32[3,8192]{1,0:T(4,128)}, f32[3,8192]{1,0:T(4,128)}, u32[]{:S(2)}, u32[]{:S(2)}) collective-permute-start(f32[3,8192]{1,0:T(4,128)} %param.17), channel_id=1, source_target_pairs={{0,2},{2,4},{4,6},{6,8},{8,10},{10,12},{12,14},{1,3},{3,5},{5,7},{... | collective-permute-start | bytes 294920 | tf_op jit(solution)/shard_map/ppermute | solution.py:18
  15.8 7.0 %copy-start.7 = (f32[3,8192]{1,0:T(4,128)S(1)}, f32[3,8192]{1,0:T(4,128)}, u32[]{:S(2)}) copy-start(f32[3,8192]{1,0:T(4,128)} %param.17) | copy-start | bytes 294916
  15.8 7.9 %copy-start.19 = (s32[2,3]{1,0:T(2,128)S(1)}, s32[2,3]{1,0:T(2,128)}, u32[]{:S(2)}) copy-start(s32[2,3]{1,0:T(2,128)} %param.24) | copy-start | bytes 76
  17.9 45.2 %copy-start.3 = (bf16[32,128,64]{2,1,0:T(8,128)(2,1)}, bf16[32,128,64]{2,1,0:T(8,128)(2,1)S(1)}, u32[]{:S(2)}) copy-start(bf16[32,128,64]{2,1,0:T(8,128)(2,1)S(1)} %reshape.843) | copy-start | bytes 1572868
  17.9 43.6 %copy-start.12 = (f32[3,32]{1,0:T(4,128)S(1)}, f32[3,32]{1,0:T(4,128)}, u32[]{:S(2)}) copy-start(f32[3,32]{1,0:T(4,128)} %param.20) | copy-start | bytes 1156
  17.9 45.2 %copy-start.14 = (s32[16,12]{1,0:T(8,128)S(1)}, s32[16,12]{1,0:T(8,128)}, u32[]{:S(2)}) copy-start(s32[16,12]{1,0:T(8,128)} %param.23) | copy-start | bytes 2308
  18.9 41.7 %copy-start.15 = (s32[128,27]{0,1:T(8,128)S(1)}, s32[128,27]{0,1:T(8,128)}, u32[]{:S(2)}) copy-start(s32[128,27]{0,1:T(8,128)} %param.21) | copy-start | bytes 41476
  18.9 44.9 %copy-start.13 = (s32[128,64]{0,1:T(8,128)S(1)}, s32[128,64]{0,1:T(8,128)}, u32[]{:S(2)}) copy-start(s32[128,64]{0,1:T(8,128)} %param.22) | copy-start | bytes 98308
  21.5 246.4 %collective-permute-start.5 = (f32[144,512]{0,1:T(8,128)}, f32[144,512]{0,1:T(8,128)}, u32[]{:S(2)}, u32[]{:S(2)}) collective-permute-start(f32[144,512]{0,1:T(8,128)} %bitcast.38), channel_id=1, source_target_pairs={{2,0},{4,2},{6,4},{8,6},{10,8},{12,10},{14,12},{3,1},{5,3},{7,5},{... | collective-permute-start | bytes 884744 | tf_op jit(solution)/shard_map/ppermute | solution.py:21
  23.6 80.1 %copy-start.6 = (bf16[16,8192]{1,0:T(8,128)(2,1)S(1)}, bf16[16,8192]{1,0:T(8,128)(2,1)}, u32[]{:S(2)}) copy-start(bf16[16,8192]{1,0:T(8,128)(2,1)} %param.16) | copy-start | bytes 786436
  66.9 201.0 %collective-permute-start.4 = (f32[144,512]{0,1:T(8,128)}, f32[144,512]{0,1:T(8,128)}, u32[]{:S(2)}, u32[]{:S(2)}) collective-permute-start(f32[144,512]{0,1:T(8,128)} %bitcast.38), channel_id=1, source_target_pairs={{0,2},{2,4},{4,6},{6,8},{8,10},{10,12},{12,14},{1,3},{3,5},{5,7},{... | collective-permute-start | bytes 884744 | tf_op jit(solution)/shard_map/ppermute | solution.py:18
  112.3 5.0 copy-start.1
  119.5 1.9 copy-start.2
  132.1 5.0 copy-start.1
  139.3 1.9 copy-start.2
  151.9 5.0 copy-start.1
  159.1 1.9 copy-start.2
  171.7 5.0 copy-start.1
  178.9 1.9 copy-start.2
  191.5 5.0 copy-start.1
  198.7 1.9 copy-start.2
  211.3 5.0 copy-start.1
  218.5 1.9 copy-start.2
  231.1 5.0 copy-start.1
  250.9 5.0 copy-start.1
  258.1 1.9 copy-start.2
  278.5 4.3 copy-start.4
  595.9 4.4 copy-start.5
  (8 other events, 10.0 us)
where the time goes:
time: 605 us; the launch traced here: 601 us
  local copies, waits for them, and re-layouts  327 us (54%)
  matrix products  161 us (27%)
  blocking collectives  54.9 us (9%)
  other arithmetic  39 us (6%)
  starting transfers between devices  18.4 us (3%)
    gather x19, local copies, waits for them, and re-layouts, couple_one_block(): coefficients[local_rows]  147 us
    dot_general x11, matrix products, couple_one_block(): jnp.einsum('bfrs,bfsv->brv', weights, coefficients[local_rows], precision...  111 us
    reshape x16, local copies, waits for them, and re-layouts, near_one_block(): source_values[:, local_rows]  47.6 us
    gather x23, local copies, waits for them, and re-layouts, couple_one_block(): far_centres = centres[:, local_rows]  44.1 us
    dot_general x8, matrix products, near_one_block(): jnp.einsum('bpm,wbm->wbp', weights, values, preferred_element_type=jnp.fl...  41.2 us
    all_gather x1, blocking collectives, body(): lax.all_gather(root_flat, ('leaf', 'sub'), axis=0, tiled=True)  36.2 us
    gather x16, local copies, waits for them, and re-layouts, near_one_block(): source_points[:, local_rows]  19 us
    all_gather x1, blocking collectives, body(): lax.all_gather(root_centre, ('leaf', 'sub'), axis=1, tiled=True)  18.6 us
  transfers between devices with their start and end apart: 6, of which 0 were waited for; matrix products, arithmetic and copies ran while one was open for 32% of the time, Pallas kernels for 0%

commit v1 on v0

v1 whole, which is shorter than its diff:
```python
import functools
import math

import jax
import jax.numpy as jnp
import numpy as np
from jax import lax
from jax.experimental import pallas as pl
from jax.experimental.pallas import tpu as pltpu
from jax.sharding import PartitionSpec as P

F32 = jnp.float32
BF16 = jnp.bfloat16
SCALE = 4.0 * math.pi
SOFT = (SCALE * 0.25) ** 2
HI = lax.Precision.HIGHEST
NN = (((1,), (0,)), ((), ()))
NT = (((1,), (1,)), ((), ()))
PAIRS = 16
ROW_X, ROW_P, ROW_C, ROW_MH, ROW_ML, ROW_K, ROWS = 0, 256, 512, 1024, 1088, 1152, 1168
UNEAR = 8
UFAR = 8


def dot(a, b, dims=NN, precision=None):
    return lax.dot_general(a, b, dims, precision=precision, preferred_element_type=F32)


def iota(shape, dim):
    return lax.broadcasted_iota(jnp.int32, shape, dim)


def rounded(x):
    return x.astype(BF16).astype(F32)


def pieces(x):
    high = rounded(x)
    rest = x - high
    mid = rounded(rest)
    return high, mid, rounded(rest - mid)


def rows8(x3):
    zero = jnp.zeros((1, x3.shape[1]), F32)
    return jnp.concatenate([x3, zero, x3, zero], axis=0)


def pack16(x8):
    high, mid, low = pieces(x8)
    first = jnp.where(iota(x8.shape, 0) < 4, high, mid)
    return jnp.concatenate([first, low], axis=0).astype(BF16)


def unpack16(x16):
    x16 = x16.astype(F32)
    first, low = x16[:8], x16[8:]
    return first + pltpu.roll(first, 4, 0) + low


def with_norm(u8, extra):
    square = u8 * u8
    norm = pltpu.roll(square, 1, 0) + pltpu.roll(square, 2, 0) + pltpu.roll(square, 3, 0)
    return jnp.where(iota(u8.shape, 0) % 4 == 3, norm + extra, u8)


def source_rows(u8):
    high, mid, low = pieces(with_norm(u8, 0.0))
    row = iota(u8.shape, 0)
    a = jnp.where(row < 4, high, mid)
    b = jnp.where(row % 4 == 3, 1.0, a)
    c = jnp.where(row < 4, low, jnp.where(row == 7, 1.0, high))
    return jnp.concatenate([a, b, c, jnp.zeros_like(a)], axis=0)


def target_rows(u8):
    high, mid, low = pieces(with_norm(u8, SOFT))
    row = iota(u8.shape, 0)
    a = jnp.where(row % 4 == 3, 1.0, -2.0 * high)
    b = jnp.where(row == 3, high, jnp.where(row == 7, mid, -2.0 * mid))
    c = jnp.where(
        row < 3,
        -2.0 * high,
        jnp.where(row == 3, 1.0, jnp.where(row == 7, low, -2.0 * low)),
    )
    return jnp.concatenate([a, b, c, jnp.zeros_like(a)], axis=0)


def eye(n):
    return (iota((n, n), 0) == iota((n, n), 1)).astype(BF16)


def turned(rows32, identity):
    return dot(identity, rows32.astype(BF16), NT).astype(BF16)


def origin8(base):
    out = []
    for axis in range(3):
        cell = jnp.int32(0)
        for bit in range(8):
            cell = cell + ((base >> (3 * bit + axis)) & 1) * (1 << bit)
        out.append(cell.astype(F32) + (4.0 if axis == 0 else 2.0))
    row = iota((8, 128), 0) % 4
    return jnp.where(
        row == 0, out[0], jnp.where(row == 1, out[1], jnp.where(row == 2, out[2], 0.0))
    )


def four_tiled(nat, group):
    turns = [nat] + [pltpu.roll(nat, 32 * k, 1) for k in (1, 2, 3)]
    out = []
    for h in range(4):
        pick = [turns[(q - h) % 4] for q in range(4)]
        out.append(
            jnp.where(
                group < 2,
                jnp.where(group == 0, pick[0], pick[1]),
                jnp.where(group == 2, pick[2], pick[3]),
            )
        )
    return out


def expand_centres(c8, tiles):
    spread = (iota((128, 128), 0) == iota((128, 128), 1) // 32).astype(F32)
    stack = [c8 if t == 0 else pltpu.roll(c8, 128 - 4 * t, 1) for t in range(tiles)]
    return dot(jnp.concatenate(stack, axis=0), spread, precision=HI)


def diagonal_basis(basis):
    leaf = iota((32, 256), 1) // 64
    zero = jnp.zeros_like(basis)
    return jnp.concatenate([jnp.where(leaf == h, basis, zero) for h in range(4)], axis=0)


def items_of(counts, slots):
    groups = jnp.floor((counts + (slots - 1)) * (1.0 / slots))
    wide = jnp.broadcast_to(groups, (128, 128))
    lower = (iota((128, 128), 1) <= iota((128, 128), 0)).astype(BF16)
    ends = dot(lower, wide.astype(BF16))
    out = []
    for t in range(8):
        k = (iota((128, 128), 1) + 128 * t).astype(F32)
        passed = jnp.where(ends <= k, 1.0, 0.0)
        leaf = jnp.sum(passed, axis=0, keepdims=True)
        start = jnp.sum(passed * wide, axis=0, keepdims=True)
        group = jnp.where(leaf >= 128.0, 0.0, k[:1] - start)
        out.append(leaf * 16.0 + group)
    out = jnp.concatenate(out + [ends[127:128]], axis=0)
    return jnp.concatenate([out, jnp.zeros((7, 128), F32)], axis=0).astype(jnp.int32)


def local_kernel(
    dev_ref,
    pair_ref,
    vec_ref,
    pts_ref,
    basis_ref,
    transfer_ref,
    near_ref,
    far_ref,
    ahead_ref,
    back_ref,
    root_ref,
    coef_ref,
    mid_ref,
    centre_ref,
    near_items_ref,
    far_items_ref,
    near_out_ref,
    far_out_ref,
    p8_ref,
):
    dev = dev_ref[0]
    base = dev * 128
    lane = iota((8, 128), 1)
    group = iota((16, 128), 1) // 32
    near = near_ref[...]
    far = far_ref[...]
    near_items_ref[...] = items_of(
        jnp.sum(jnp.where(near >= 0, 1.0, 0.0), axis=1, keepdims=True), 4
    )
    far_items_ref[...] = items_of(
        jnp.sum(jnp.where(far >= 0, 1.0, 0.0), axis=1, keepdims=True), 8
    )
    near_out_ref[...] = jnp.full(near_out_ref.shape, 384, jnp.int32)
    near_out_ref[0:128, 0 : near.shape[1]] = jnp.where(near >= 0, near - base + 128, 384)
    far_out_ref[...] = jnp.full(far_out_ref.shape, 384, jnp.int32)
    far_out_ref[0:128, 0 : far.shape[1]] = jnp.where(far >= 0, far - base + 128, 384)
    mids = []
    four_e = jnp.concatenate([transfer_ref[...]] * 4, axis=1)
    rows = []
    for t in range(32):
        cols = slice(256 * t, 256 * t + 256)
        nat = dot(vec_ref[:, cols], diagonal_basis(basis_ref[:, cols]), NT)
        coef_ref[16 * t : 16 * t + 16, :] = nat.astype(BF16)
        rows.append(nat)
    stack = jnp.concatenate(
        [jnp.concatenate([rows[2 * m], rows[2 * m + 1]], axis=1) for m in range(16)], axis=0
    )
    mids = dot(stack, four_e, precision=HI)
    mid_nat = []
    for t in range(4):
        part = [mids[16 * (4 * t + h) : 16 * (4 * t + h) + 16] for h in range(4)]
        mid_nat.append(
            jnp.where(
                group < 2,
                jnp.where(group == 0, part[0], part[1]),
                jnp.where(group == 2, part[2], part[3]),
            )
        )
    roots = dot(
        jnp.concatenate(
            [jnp.concatenate([mid_nat[0], mid_nat[1]], axis=1),
             jnp.concatenate([mid_nat[2], mid_nat[3]], axis=1)], axis=0),
        four_e,
        precision=HI,
    )
    root_ref[0:32, :] = roots
    for t in range(4):
        high = mid_nat[t].astype(BF16)
        mid_ref[16 * t : 16 * t + 16, :] = high
        mid_ref[64 + 16 * t : 64 + 16 * t + 16, :] = (mid_nat[t] - high.astype(F32)).astype(BF16)
    c8 = jnp.zeros((8, 128), F32)
    for t in range(64):
        p8 = rows8(pts_ref[:, 128 * t : 128 * t + 128])
        p8_ref[:, 128 * t : 128 * t + 128] = p8
        total = p8
        for shift in (32, 16, 8, 4, 2, 1):
            total = total + pltpu.roll(total, 128 - shift, 1)
        even = pltpu.roll(total, 2 * t, 1) if t else total
        odd = pltpu.roll(total, (2 * t + 1 + 64) % 128, 1)
        c8 = jnp.where(lane == 2 * t, even, jnp.where(lane == 2 * t + 1, odd, c8))
    c8 = c8 * (1.0 / 64.0)
    centre_ref[...] = pack16(c8)
    for b in range(2):
        mean = jnp.sum(jnp.where(lane // 64 == b, c8, 0.0), axis=1, keepdims=True) * (1.0 / 64.0)
        root_ref[32 + 8 * b : 40 + 8 * b, :] = jnp.broadcast_to(mean, (8, 128))
    for way, msg_ref in enumerate((ahead_ref, back_ref)):
        for k in range(PAIRS):
            at = pl.multiple_of(pair_ref[dev, way * PAIRS + k] * 128, 128)
            msg_ref[ROW_X + 16 * k : ROW_X + 16 * k + 16, :] = vec_ref[:, pl.ds(at, 128)]
            msg_ref[ROW_P + 16 * k : ROW_P + 16 * k + 16, :] = pack16(p8_ref[:, pl.ds(at, 128)])
        msg_ref[ROW_C : ROW_C + 512, :] = coef_ref[...]
        msg_ref[ROW_MH : ROW_MH + 128, :] = mid_ref[...]
        msg_ref[ROW_K : ROW_K + 16, :] = centre_ref[...]


def near_kernel(
    dev_ref,
    item_ref,
    list_ref,
    map_ref,
    vec_ref,
    pts_ref,
    prev_ref,
    next_ref,
    out_ref,
    table_ref,
    target_ref,
    sum_ref,
):
    dev = dev_ref[0]
    origin = origin8(dev * 128)
    identity = eye(128)
    low = iota((48, 128), 1) < 64

    def put(row, x, rows):
        both = jnp.concatenate([x.astype(F32), rows], axis=0)
        other = pltpu.roll(both, 64, 1)
        table_ref[row] = jnp.where(low, both, other).astype(BF16)
        table_ref[row + 1] = jnp.where(low, other, both).astype(BF16)

    for t in range(64):
        cols = slice(128 * t, 128 * t + 128)
        u8 = (rows8(pts_ref[:, cols]) - origin) * SCALE
        u8 = jnp.where(iota((8, 128), 0) % 4 == 3, 0.0, u8)
        put(2 * t, vec_ref[:, cols], source_rows(u8))
        turn = turned(target_rows(u8), identity)
        target_ref[2 * t] = turn[:64]
        target_ref[2 * t + 1] = turn[64:]
    for way, msg_ref in enumerate((prev_ref, next_ref)):
        for k in range(PAIRS):
            p8 = unpack16(msg_ref[ROW_P + 16 * k : ROW_P + 16 * k + 16, :])
            u8 = (p8 - origin) * SCALE
            put(
                128 + 2 * (PAIRS * way + k),
                msg_ref[ROW_X + 16 * k : ROW_X + 16 * k + 16, :],
                source_rows(u8),
            )
    table_ref[192] = jnp.where(iota((48, 128), 0) < 16, 0.0, table_ref[0].astype(F32)).astype(BF16)
    target_ref[128] = target_ref[0]
    sum_ref[...] = jnp.zeros_like(sum_ref)

    def step(it, carry):
        for u in range(UNEAR):
            k = it * UNEAR + u
            packed = item_ref[k >> 7, k & 127]
            leaf = packed >> 4
            col = (packed & 15) * 4
            part = [table_ref[map_ref[dev, list_ref[leaf, col + s]]] for s in range(4)]
            both = jnp.concatenate(
                [jnp.where(low, part[0], part[1]), jnp.where(low, part[2], part[3])], axis=1
            )
            squared = dot(target_ref[leaf], both[16:])
            weights = lax.rsqrt(squared).astype(BF16)
            sum_ref[leaf] += dot(both[:16], weights, NT)
        return carry

    lax.fori_loop(0, (item_ref[8, 0] + (UNEAR - 1)) // UNEAR, step, 0)
    for t in range(64):
        out_ref[:, 128 * t : 128 * t + 128] = jnp.concatenate(
            [sum_ref[2 * t], sum_ref[2 * t + 1]], axis=1
        )


def top_kernel(n_sub, dev_ref, transfer_ref, *refs):
    root_refs, out_ref = refs[:n_sub], refs[n_sub]
    sub = lax.rem(dev_ref[0], n_sub)
    coef = jnp.zeros((16, 128), F32)
    centre = jnp.zeros((8, 128), F32)
    for k in range(n_sub):
        owner = lax.rem(sub + n_sub - k, n_sub)
        for b in range(2):
            c = lax.rem(owner * 2 + b, 8)
            e = transfer_ref[pl.ds(pl.multiple_of(c * 32, 32), 32), :]
            e4 = jnp.concatenate([e] * 4, axis=1)
            coef = coef + dot(root_refs[k][16 * b : 16 * b + 16, 0:32], e4, precision=HI)
            centre = centre + root_refs[k][32 + 8 * b : 40 + 8 * b, :]
    out_ref[0:16, :] = coef
    out_ref[16:24, :] = centre * (1.0 / (2 * n_sub))


def far_kernel(
    n_sub,
    n_leaf,
    dev_ref,
    item_ref,
    list_ref,
    mid_list_ref,
    root_list_ref,
    top_list_ref,
    near_ref,
    basis_ref,
    transfer_ref,
    proxy_ref,
    coef_ref,
    mid_ref,
    centre_ref,
    prev_ref,
    next_ref,
    *refs,
):
    root_refs = refs[:n_sub]
    top_refs = refs[n_sub : n_sub + n_leaf]
    out_ref, table_ref, target_ref, sum_ref, mtable_ref, mtarget_ref, mout_ref, small_ref = refs[
        n_sub + n_leaf :
    ]
    dev = dev_ref[0]
    sub = lax.rem(dev, n_sub)
    top = lax.div(dev, n_sub)
    origin = origin8(dev * 128)
    identity = eye(128)
    proxy8 = rows8(jnp.concatenate([proxy_ref[...]] * 4, axis=1))
    group64 = iota((64, 128), 1) // 32
    group48 = iota((48, 128), 1) // 32
    f3 = iota((8, 128), 0) % 4 == 3

    def shifted(c8, radius):
        return jnp.where(f3, 0.0, (c8 - origin + radius * proxy8) * SCALE)

    mean8 = jnp.where(iota((128, 128), 0) // 8 == iota((128, 128), 1), 0.125, 0.0)
    own_c8 = None
    for way, block in enumerate((prev_ref, None, next_ref)):
        packed = centre_ref[...] if way == 1 else block[ROW_K : ROW_K + 16, :]
        c8 = unpack16(packed)
        spread = expand_centres(c8, 32)
        for t in range(32):
            u8 = shifted(spread[8 * t : 8 * t + 8], 1.0)
            at = slice(16 * t, 16 * t + 16)
            coef = coef_ref[at, :] if way == 1 else block[ROW_C + 16 * t : ROW_C + 16 * t + 16, :]
            tiles = four_tiled(
                jnp.concatenate([coef.astype(F32), source_rows(u8)], axis=0), group48
            )
            for h in range(4):
                table_ref[128 * way + 4 * t + h] = tiles[h].astype(BF16)
            if way == 1:
                turn = turned(target_rows(u8), identity)
                for h in range(4):
                    target_ref[4 * t + h] = turn[32 * h : 32 * h + 32]
        m8 = dot(c8, mean8, precision=HI)
        spread = expand_centres(m8, 4)
        for t in range(4):
            u8 = shifted(spread[8 * t : 8 * t + 8], 2.0)
            if way == 1:
                high = mid_ref[16 * t : 16 * t + 16, :]
                rest = mid_ref[64 + 16 * t : 64 + 16 * t + 16, :]
            else:
                high = block[ROW_MH + 16 * t : ROW_MH + 16 * t + 16, :]
                rest = block[ROW_ML + 16 * t : ROW_ML + 16 * t + 16, :]
            tiles = four_tiled(
                jnp.concatenate([high.astype(F32), rest.astype(F32), source_rows(u8)], axis=0),
                group64,
            )
            for h in range(4):
                mtable_ref[16 * way + 4 * t + h] = tiles[h].astype(BF16)
            if way == 1:
                turn = turned(target_rows(u8), identity)
                for h in range(4):
                    mtarget_ref[4 * t + h] = turn[32 * h : 32 * h + 32]
    table_ref[384] = jnp.where(iota((48, 128), 0) < 16, 0.0, table_ref[128].astype(F32)).astype(BF16)
    mtable_ref[48] = jnp.where(iota((64, 128), 0) < 32, 0.0, mtable_ref[16].astype(F32)).astype(BF16)
    target_ref[128] = target_ref[0]
    sum_ref[...] = jnp.zeros_like(sum_ref)

    def step(it, carry):
        for u in range(UFAR):
            k = it * UFAR + u
            packed = item_ref[k >> 7, k & 127]
            leaf = packed >> 4
            col = (packed & 15) * 8
            part = [table_ref[list_ref[leaf, col + s]] for s in range(8)]
            both = jnp.concatenate(
                [
                    jnp.where(
                        group48 < 2,
                        jnp.where(group48 == 0, part[h], part[h + 1]),
                        jnp.where(group48 == 2, part[h + 2], part[h + 3]),
                    )
                    for h in (0, 4)
                ],
                axis=1,
            )
            squared = dot(target_ref[leaf], both[16:])
            weights = lax.rsqrt(squared).astype(BF16)
            sum_ref[leaf] += dot(both[:16], weights, NT)
        return carry

    lax.fori_loop(0, (item_ref[8, 0] + (UFAR - 1)) // UFAR, step, 0)

    def couple(target, rows, table):
        while len(rows) % 4:
            rows.append(jnp.int32(-1))
        tiles = []
        for h in range(0, len(rows), 4):
            part = [table(r) for r in rows[h : h + 4]]
            tiles.append(
                jnp.where(
                    group64 < 2,
                    jnp.where(group64 == 0, part[0], part[1]),
                    jnp.where(group64 == 2, part[2], part[3]),
                )
            )
        both = jnp.concatenate(tiles, axis=1) if len(tiles) > 1 else tiles[0]
        weights = lax.rsqrt(dot(target, both[32:]))
        high = weights.astype(BF16)
        rest = (weights - high.astype(F32)).astype(BF16)
        first = dot(both[:32], high, NT)
        return first[:16] + first[16:] + dot(both[:16], rest, NT)

    def fill(slot, coef, u8):
        high = rounded(coef)
        small_ref[slot] = jnp.concatenate([high, coef - high, source_rows(u8)], axis=0).astype(BF16)

    empty_top, first_root = n_leaf, n_leaf + 1
    empty_root = first_root + 2 * n_sub
    blank = jnp.zeros((16, 128), F32)
    for k in range(n_leaf):
        fill(k, top_refs[k][0:16, :], shifted(top_refs[k][16:24, :], 8.0))
    fill(empty_top, blank, shifted(top_refs[0][16:24, :], 8.0))
    for k in range(n_sub):
        for b in range(2):
            fill(
                first_root + 2 * k + b,
                root_refs[k][16 * b : 16 * b + 16, :],
                shifted(root_refs[k][32 + 8 * b : 40 + 8 * b, :], 4.0),
            )
    fill(empty_root, blank, shifted(root_refs[0][32:40, :], 4.0))

    rows = []
    for s in range(top_list_ref.shape[1]):
        j = top_list_ref[top, s]
        rows.append(jnp.where(j >= 0, lax.rem(top - j + n_leaf, n_leaf), -1))
    target = turned(target_rows(shifted(top_refs[0][16:24, :], 8.0)), identity)[:32]
    top_out = couple(target, rows, lambda r: small_ref[jnp.where(r >= 0, r, empty_top)])
    root_out = []
    for b in range(2):
        rows = []
        for s in range(root_list_ref.shape[1]):
            j = root_list_ref[b, s]
            inside = j - top * (2 * n_sub)
            shift = lax.rem(sub - (inside >> 1) + n_sub, n_sub)
            rows.append(jnp.where(j >= 0, 2 * shift + (inside & 1), -1))
        target = turned(
            target_rows(shifted(root_refs[0][32 + 8 * b : 40 + 8 * b, :], 4.0)), identity
        )[:32]
        far_in = couple(
            target, rows, lambda r: small_ref[jnp.where(r >= 0, first_root + r, empty_root)]
        )
        c = lax.rem(sub * 2 + b, 8)
        e = transfer_ref[pl.ds(pl.multiple_of(c * 32, 32), 32), :]
        root_out.append(far_in + dot(top_out, e, NT, HI))
    for b in range(2):
        down = dot(root_out[b], transfer_ref[...], NT, HI)
        for c in range(8):
            m = 8 * b + c
            rows = []
            for s in range(mid_list_ref.shape[1]):
                j = mid_list_ref[m, s]
                rows.append(jnp.where(j >= 0, j - dev * 16 + 16, -1))
            far_in = couple(
                mtarget_ref[m], rows, lambda r: mtable_ref[jnp.where(r >= 0, r, 48)]
            )
            mout_ref[16 * m : 16 * m + 16, :] = far_in + down[:, 32 * c : 32 * c + 32]
    down = dot(mout_ref[...], transfer_ref[...], NT, HI)
    for m in range(16):
        for half in range(2):
            t = 2 * m + half
            far_in = jnp.concatenate([sum_ref[4 * t + h] for h in range(4)], axis=1)
            leaf_out = far_in + down[16 * m : 16 * m + 16, 128 * half : 128 * half + 128]
            cols = slice(256 * t, 256 * t + 256)
            out_ref[:, cols] = near_ref[:, cols] + dot(
                leaf_out.astype(BF16), diagonal_basis(basis_ref[:, cols])
            )


def cells_of(index):
    out = np.zeros(index.shape + (3,), np.int64)
    for axis in range(3):
        for bit in range(8):
            out[..., axis] |= ((index >> (3 * bit + axis)) & 1) << bit
    return out


@functools.cache
def near_plan(devices, leaves):
    pairs = np.zeros((devices, 2 * PAIRS), np.int32)
    for dev in range(devices):
        own = cells_of(np.arange(leaves) + dev * leaves)
        for way, other in ((0, dev + 1), (1, dev - 1)):
            if not 0 <= other < devices:
                continue
            theirs = cells_of(np.arange(leaves) + other * leaves)
            low, high = theirs.min(0) - 1, theirs.max(0) + 1
            touch = ((own >= low) & (own <= high)).all(1)
            found = np.unique(np.nonzero(touch)[0] // 2)
            assert len(found) <= PAIRS
            pairs[dev, way * PAIRS : way * PAIRS + len(found)] = found
    rows = np.full((devices, 3 * leaves + 1), 192, np.int32)
    for dev in range(devices):
        rows[dev, leaves : 2 * leaves] = np.arange(leaves)
        for way, other, first in ((0, dev - 1, 0), (1, dev + 1, 2 * leaves)):
            if not 0 <= other < devices:
                continue
            for k in reversed(range(PAIRS)):
                pair = pairs[other, way * PAIRS + k]
                for odd in range(2):
                    rows[dev, first + 2 * pair + odd] = 128 + 2 * (PAIRS * way + k) + odd
    return pairs, rows


def around(x, axis, count):
    out = [x]
    for k in range(1, count):
        out.append(lax.ppermute(x, axis, [(i, (i + k) % count) for i in range(count)]))
    return out


SMEM = pl.BlockSpec(memory_space=pltpu.SMEM)
VMEM = pl.BlockSpec(memory_space=pltpu.VMEM)


def call(kernel, name, in_specs, outs, scratch, cost):
    return pl.pallas_call(
        kernel,
        name=name,
        in_specs=in_specs,
        out_shape=outs,
        out_specs=jax.tree.map(lambda _: VMEM, outs),
        scratch_shapes=scratch,
        compiler_params=pltpu.CompilerParams(vmem_limit_bytes=48 << 20),
        cost_estimate=pl.CostEstimate(flops=cost, bytes_accessed=1 << 20, transcendentals=0),
    )


def body(
    vectors,
    points,
    leaf_basis,
    transfer,
    proxy_points,
    near_list,
    far_leaf,
    far_mid,
    far_root,
    far_top,
):
    shape = jax.ShapeDtypeStruct
    n_sub, n_leaf = lax.axis_size("sub"), lax.axis_size("leaf")
    devices = n_sub * n_leaf
    along = ("leaf", "sub")
    device = lax.axis_index(along).astype(jnp.int32).reshape(1)
    pairs, near_rows = near_plan(devices, near_list.shape[0])
    matrices = transfer.reshape(256, 32)
    ahead, back, roots, coef, mid, centre, near_items, far_items, near_local, far_local = call(
        local_kernel,
        "local",
        [SMEM, SMEM] + [VMEM] * 6,
        (
            shape((ROWS, 128), BF16),
            shape((ROWS, 128), BF16),
            shape((48, 128), F32),
            shape((512, 128), BF16),
            shape((128, 128), BF16),
            shape((16, 128), BF16),
            shape((16, 128), jnp.int32),
            shape((16, 128), jnp.int32),
            shape((136, 28), jnp.int32),
            shape((136, 64), jnp.int32),
        ),
        [pltpu.VMEM((8, 8192), F32)],
        1 << 30,
    )(device, jnp.asarray(pairs), vectors, points, leaf_basis, matrices, near_list, far_leaf)
    from_prev = lax.ppermute(ahead, along, [(i, i + 1) for i in range(devices - 1)])
    from_next = lax.ppermute(back, along, [(i + 1, i) for i in range(devices - 1)])
    row_roots = around(roots, "sub", n_sub)
    top = call(
        functools.partial(top_kernel, n_sub),
        "top",
        [SMEM] + [VMEM] * (1 + n_sub),
        shape((24, 128), F32),
        [],
        1 << 20,
    )(device, matrices, *row_roots)
    tops = around(top, "leaf", n_leaf)
    near = call(
        near_kernel,
        "near",
        [SMEM] * 4 + [VMEM] * 4,
        shape((16, 8192), F32),
        [
            pltpu.VMEM((193, 48, 128), BF16),
            pltpu.VMEM((129, 64, 32), BF16),
            pltpu.VMEM((129, 16, 64), F32),
        ],
        1 << 33,
    )(device, near_items, near_local, jnp.asarray(near_rows), vectors, points, from_prev, from_next)
    return call(
        functools.partial(far_kernel, n_sub, n_leaf),
        "far",
        [SMEM] * 6 + [VMEM] * (9 + n_sub + n_leaf),
        shape((16, 8192), F32),
        [
            pltpu.VMEM((385, 48, 128), BF16),
            pltpu.VMEM((129, 32, 32), BF16),
            pltpu.VMEM((129, 16, 32), F32),
            pltpu.VMEM((49, 64, 128), BF16),
            pltpu.VMEM((16, 32, 32), BF16),
            pltpu.VMEM((256, 32), F32),
            pltpu.VMEM((n_leaf + 2 + 2 * n_sub, 64, 128), BF16),
        ],
        1 << 33,
    )(
        device,
        far_items,
        far_local,
        far_mid,
        far_root,
        far_top,
        near,
        leaf_basis,
        matrices,
        proxy_points,
        coef,
        mid,
        centre,
        from_prev,
        from_next,
        *row_roots,
        *tops,
    )


def solution(mesh):
    return jax.shard_map(
        body,
        mesh=mesh,
        in_specs=(
            P("vec", ("groups", "leaf", "sub")),
            P(None, ("groups", "leaf", "sub")),
            P(None, ("groups", "leaf", "sub")),
            P(),
            P(),
            P(("groups", "leaf", "sub"), None),
            P(("groups", "leaf", "sub"), None),
            P(("groups", "leaf", "sub"), None),
            P(("groups", "leaf", "sub"), None),
            P("groups", None),
        ),
        out_specs=P("vec", ("groups", "leaf", "sub")),
        check_vma=False,
    )
```

time: 605 us -> 130 us (0.21)
  local copies, waits for them, and re-layouts: 327 us -> 5.95 us
  matrix products: 161 us -> 0 us
  Pallas kernels: 0 us -> 98.7 us
  blocking collectives: 54.9 us -> 0 us
  other arithmetic: 39 us -> 0 us
  waiting for transfers between devices: 0.02 us -> 9.24 us
    gather x67 -> x0, local copies, waits for them, and re-layouts: 228 us -> none  [the longest x19 147 us: couple_one_block(): coefficients[local_rows]]
    dot_general x28 -> x0, matrix products: 161 us -> none  [the longest x11 111 us: couple_one_block(): jnp.einsum('bfrs,bfsv->brv', weights, coefficients[local_rows], precision...]
    pallas_call x0 -> x4, Pallas kernels: none -> 98.7 us  [the longest x1 58.6 us: body(): call(functools.partial(far_kernel, n_sub, n_leaf), 'far', [SMEM] * 6 + [V...]
    reshape x27 -> x0, local copies, waits for them, and re-layouts: 57.7 us -> none  [the longest x16 47.6 us: near_one_block(): source_values[:, local_rows]]
    all_gather x2 -> x0, blocking collectives: 54.9 us -> none  [the longest x1 36.2 us: body(): lax.all_gather(root_flat, ('leaf', 'sub'), axis=0, tiled=True)]
    mul x19 -> x0, other arithmetic: 12.5 us -> none  [the longest x11 6.91 us: couple_one_block(): pair_kernel(squared) * present.astype(jnp.float32)[:, :, None, None]]
    select_n x19 -> x0, other arithmetic: 11.3 us -> none  [the longest x10 5.63 us: couple_one_block(): far_centres = centres[:, local_rows]]
    dynamic_slice x17 -> x0, local copies, waits for them, and re-layouts: 11.2 us -> none  [the longest x8 5.92 us: near_field(): results = lax.map(near_one_block, (target_blocks, list_blocks))]
  transfers between devices with their start and end apart: 6 -> 6, of which waited for: 0 -> 1; matrix products, arithmetic and copies ran while one was open for 32% -> 0% of each run, Pallas kernels for 0% -> 26%
where the time goes in v1:
time: 130 us
  Pallas kernels  98.7 us (76%)
  starting transfers between devices  15.5 us (12%)
  waiting for transfers between devices  9.24 us (7%)
  local copies, waits for them, and re-layouts  5.95 us (5%)
    pallas_call x1, Pallas kernels, body(): call(functools.partial(far_kernel, n_sub, n_leaf), 'far', [SMEM] * 6 + [V...  58.6 us
    pallas_call x1, Pallas kernels, body(): call(near_kernel, 'near', [SMEM] * 4 + [VMEM] * 4, shape((16, 8192), F32)...  33.7 us
    ppermute x4, waiting for transfers between devices, around(): lax.ppermute(x, axis, [(i, (i + k) % count) for i in range(count)])  9.24 us
    ppermute x4, starting transfers between devices, around(): lax.ppermute(x, axis, [(i, (i + k) % count) for i in range(count)])  9.23 us
    pallas_call x1, Pallas kernels, body(): call(local_kernel, 'local', [SMEM, SMEM] + [VMEM] * 6, (shape((ROWS, 128)...  6.08 us
    unnamed x28, local copies, waits for them, and re-layouts  5.95 us
    ppermute x1, starting transfers between devices, body(): lax.ppermute(ahead, along, [(i, i + 1) for i in range(devices - 1)])  4.99 us
  transfers between devices with their start and end apart: 6, of which 1 were waited for; matrix products, arithmetic and copies ran while one was open for 0% of the time, Pallas kernels for 26%

profile of v1, /device:TPU:0, one launch (start us, length us, event | category | flops | bytes accessed | tf_op | source)
XLA Modules:
  0.0 129.5 jit_solution(12354730448443480220)
XLA Ops:
  0.0 0.9 copy.13.near_ref
  0.9 0.8 copy.14.far_ref
  1.7 0.0 copy-start.12
  1.7 0.7 copy-done.12
  2.4 1.0 copy-done.1
  3.4 0.9 copy-done.3
  4.4 0.9 copy-done.5
  5.3 6.1 %local.1 = (bf16[1168,128]{1,0:T(8,128)(2,1)S(1)}, bf16[1168,128]{1,0:T(8,128)(2,1)S(1)}, f32[48,128]{1,0:T(8,128)S(1)}, bf16[512,128]{1,0:T(8,128)(2,1)S(1)}, b...) custom-call(s32[1]{0:T(128)} %bitcast.dev_ref, ...), custom_call_target="tpu_custom_call" | custom-call | flops 1073741824 | bytes 1048576 | tf_op jit(solution)/shard_map/local/pallas_call | solution.py:606
  11.4 5.0 %collective-permute-start = (bf16[1168,128]{1,0:T(8,128)(2,1)S(1)}, bf16[1168,128]{1,0:T(8,128)(2,1)S(1)}, u32[]{:S(2)}, u32[]{:S(2)}) collective-permute-start(bf16[1168,128]{1,0:T(8,128)(2,1)S(1)} %get-tuple-element.19), channel_id=1, source_target_pairs={{0,2},{2,4},{4,6},{6,8},{8,10},{10,12},{12,14},{1,3},{3,5},{5,7},{... | collective-permute-start | bytes 897032 | tf_op jit(solution)/shard_map/ppermute | solution.py:625
  16.4 1.3 collective-permute-start.1
  17.7 0.0 copy-start.11
  17.7 2.7 %collective-permute-start.2 = (f32[48,128]{1,0:T(8,128)S(1)}, f32[48,128]{1,0:T(8,128)S(1)}, u32[]{:S(2)}, u32[]{:S(2)}) collective-permute-start(f32[48,128]{1,0:T(8,128)S(1)} %get-tuple-element.24.refs_0_), channel_id=1, source_target_pairs={{0,2},{2,0},{1,3},{3,1},{4,6},{6,4},{5,7},{7,5},{8,10},{10,8},{9,1... | collective-permute-start | bytes 73736 | tf_op jit(solution)/shard_map/ppermute | solution.py:566
  20.4 9.2 %collective-permute-done.2.refs_1_ = f32[48,128]{1,0:T(8,128)S(1)} collective-permute-done((f32[48,128]{1,0:T(8,128)S(1)}, f32[48,128]{1,0:T(8,128)S(1)}, u32[]{:S(2)}, u32[]{:S(2)}) %collective-permute-start.2) | collective-permute-done | bytes 24608 | tf_op jit(solution)/shard_map/ppermute | solution.py:566
  29.6 0.3 top.1.refs_2_
  29.9 5.5 %collective-permute-start.5 = (f32[24,128]{1,0:T(8,128)S(1)}, f32[24,128]{1,0:T(8,128)S(1)}, u32[]{:S(2)}, u32[]{:S(2)}) collective-permute-start(f32[24,128]{1,0:T(8,128)S(1)} %top.1.refs_2_), channel_id=1, source_target_pairs={{0,12},{4,0},{8,4},{12,8},{1,13},{5,1},{9,5},{13,9},{2,14},{6,2},{... | collective-permute-start | bytes 36872 | tf_op jit(solution)/shard_map/ppermute | solution.py:566
  35.4 0.0 collective-permute-start.4
  35.4 1.0 collective-permute-start.3
  36.4 0.0 collective-permute-done.prev_ref
  36.4 0.0 collective-permute-done.1.next_ref
  36.4 0.0 copy-done.4
  36.5 0.0 copy-start.2
  36.5 0.0 copy-start.8
  36.5 0.0 copy-start.9
  36.5 33.7 %near.1.near_ref = f32[16,8192]{1,0:T(8,128)S(1)} custom-call(s32[1]{0:T(128)} %bitcast.dev_ref, s32[16,128]{1,0:T(8,128)S(1)} %get-tuple-element.17.item_ref, s32[136,28]{1,0:T(8,128)S(1)} %get-tuple-element.18.list_ref, s32[8,385]{1,0:T(8,128)S(1)} %copy-done.11, bf16[16,8192]{1,0:T(8,128)(2,1)S(1)} %copy-done.4, f32[3,8192]{1,0:T(4,128)S(1)} %copy-done.6, ...), custom_call_target="tpu_custom_call" | custom-call | flops 8589934592 | bytes 1048576 | tf_op jit(solution)/shard_map/near/pallas_call | solution.py:637
  70.2 0.0 copy-start.7
  70.2 0.0 collective-permute-done.5.refs_5_
  70.3 0.0 collective-permute-done.4.refs_4_
  70.3 0.0 collective-permute-done.3.refs_3_
  70.3 0.0 copy-start.10
  70.3 0.6 copy-done.7
  70.9 0.0 copy-done.10
  71.0 58.6 %far.1 = f32[16,8192]{1,0:T(8,128)} custom-call(s32[1]{0:T(128)} %bitcast.dev_ref, s32[16,128]{1,0:T(8,128)S(1)} %get-tuple-element.15.item_ref, s32[136,64]{1,0:T(8,128)S(1)} %get-tuple-element.16.list_ref, s32[16,12]{1,0:T(8,128)S(1)} %copy-done.7, s32[2,3]{1,0:T(2,128)S(1)} %copy-done.10, s32[4,3]{1,0:T(4,128)S(1)} %copy-done.8, ...), custom_call_target="tpu_custom_call" | custom-call | flops 8589934592 | bytes 1048576 | tf_op jit(solution)/shard_map/far/pallas_call | solution.py:649
  (12 shorter events, 0.0 us)
Async XLA Ops:
  0.0 1.7 %copy-start = (f32[8,32,32]{2,1,0:T(8,128)S(1)}, f32[8,32,32]{2,1,0:T(8,128)}, u32[]{:S(2)}) copy-start(f32[8,32,32]{2,1,0:T(8,128)} %param.15) | copy-start | bytes 98308
  1.7 0.7 copy-start.12
  2.4 1.0 copy-start.1
  3.4 0.9 copy-start.3
  4.4 0.9 copy-start.5
  5.3 31.1 %copy-start.4 = (bf16[16,8192]{1,0:T(8,128)(2,1)S(1)}, bf16[16,8192]{1,0:T(8,128)(2,1)}, u32[]{:S(2)}) copy-start(bf16[16,8192]{1,0:T(8,128)(2,1)} %vec_ref.3) | copy-start | bytes 786436
  11.4 25.1 %copy-start.6 = (f32[3,8192]{1,0:T(4,128)S(1)}, f32[3,8192]{1,0:T(4,128)}, u32[]{:S(2)}) copy-start(f32[3,8192]{1,0:T(4,128)} %pts_ref.3) | copy-start | bytes 294916
  11.4 25.0 %collective-permute-start = (bf16[1168,128]{1,0:T(8,128)(2,1)S(1)}, bf16[1168,128]{1,0:T(8,128)(2,1)S(1)}, u32[]{:S(2)}, u32[]{:S(2)}) collective-permute-start(bf16[1168,128]{1,0:T(8,128)(2,1)S(1)} %get-tuple-element.19), channel_id=1, source_target_pairs={{0,2},{2,4},{4,6},{6,8},{8,10},{10,12},{12,14},{1,3},{3,5},{5,7},{... | collective-permute-start | bytes 897032 | tf_op jit(solution)/shard_map/ppermute | solution.py:625
  16.4 20.1 %collective-permute-start.1 = (bf16[1168,128]{1,0:T(8,128)(2,1)S(1)}, bf16[1168,128]{1,0:T(8,128)(2,1)S(1)}, u32[]{:S(2)}, u32[]{:S(2)}) collective-permute-start(bf16[1168,128]{1,0:T(8,128)(2,1)S(1)} %get-tuple-element.20), channel_id=1, source_target_pairs={{2,0},{4,2},{6,4},{8,6},{10,8},{12,10},{14,12},{3,1},{5,3},{7,5},{... | collective-permute-start | bytes 897032 | tf_op jit(solution)/shard_map/ppermute | solution.py:626
  17.7 18.8 %copy-start.11 = (s32[8,385]{1,0:T(8,128)S(1)}, s32[8,385]{1,0:T(8,128)}, u32[]{:S(2)}) copy-start(s32[8,385]{1,0:T(8,128)} %constant.16.clone.map_ref) | copy-start | bytes 36964
  17.7 11.9 %collective-permute-start.2 = (f32[48,128]{1,0:T(8,128)S(1)}, f32[48,128]{1,0:T(8,128)S(1)}, u32[]{:S(2)}, u32[]{:S(2)}) collective-permute-start(f32[48,128]{1,0:T(8,128)S(1)} %get-tuple-element.24.refs_0_), channel_id=1, source_target_pairs={{0,2},{2,0},{1,3},{3,1},{4,6},{6,4},{5,7},{7,5},{8,10},{10,8},{9,1... | collective-permute-start | bytes 73736 | tf_op jit(solution)/shard_map/ppermute | solution.py:566
  29.9 40.3 %collective-permute-start.5 = (f32[24,128]{1,0:T(8,128)S(1)}, f32[24,128]{1,0:T(8,128)S(1)}, u32[]{:S(2)}, u32[]{:S(2)}) collective-permute-start(f32[24,128]{1,0:T(8,128)S(1)} %top.1.refs_2_), channel_id=1, source_target_pairs={{0,12},{4,0},{8,4},{12,8},{1,13},{5,1},{9,5},{13,9},{2,14},{6,2},{... | collective-permute-start | bytes 36872 | tf_op jit(solution)/shard_map/ppermute | solution.py:566
  35.4 34.8 %collective-permute-start.4 = (f32[24,128]{1,0:T(8,128)S(1)}, f32[24,128]{1,0:T(8,128)S(1)}, u32[]{:S(2)}, u32[]{:S(2)}) collective-permute-start(f32[24,128]{1,0:T(8,128)S(1)} %top.1.refs_2_), channel_id=1, source_target_pairs={{0,8},{4,12},{8,0},{12,4},{1,9},{5,13},{9,1},{13,5},{2,10},{6,14},... | collective-permute-start | bytes 36872 | tf_op jit(solution)/shard_map/ppermute | solution.py:566
  35.4 34.8 %collective-permute-start.3 = (f32[24,128]{1,0:T(8,128)S(1)}, f32[24,128]{1,0:T(8,128)S(1)}, u32[]{:S(2)}, u32[]{:S(2)}) collective-permute-start(f32[24,128]{1,0:T(8,128)S(1)} %top.1.refs_2_), channel_id=1, source_target_pairs={{0,4},{4,8},{8,12},{12,0},{1,5},{5,9},{9,13},{13,1},{2,6},{6,10},{... | collective-permute-start | bytes 36872 | tf_op jit(solution)/shard_map/ppermute | solution.py:566
  36.5 33.8 %copy-start.2 = (bf16[32,8192]{1,0:T(8,128)(2,1)S(1)}, bf16[32,8192]{1,0:T(8,128)(2,1)}, u32[]{:S(2)}) copy-start(bf16[32,8192]{1,0:T(8,128)(2,1)} %basis_ref.3) | copy-start | bytes 1572868
  36.5 33.8 %copy-start.8 = (s32[4,3]{1,0:T(4,128)S(1)}, s32[4,3]{1,0:T(4,128)}, u32[]{:S(2)}) copy-start(s32[4,3]{1,0:T(4,128)} %top_list_ref.1) | copy-start | bytes 148
  36.5 33.8 %copy-start.9 = (f32[3,32]{1,0:T(4,128)S(1)}, f32[3,32]{1,0:T(4,128)}, u32[]{:S(2)}) copy-start(f32[3,32]{1,0:T(4,128)} %proxy_ref.1) | copy-start | bytes 1156
  70.2 0.7 copy-start.7
  70.3 0.7 copy-start.10
